TPU v7x, 32 devices: a whole 2x2x4 slice. The times are simulated.
32 devices in a mesh: ctx: 8 (over z, y), head: 4 (over x, core).
Axes of the slice: x: 2, y: 2, z: 4, core: 2. Of those that a mesh axis runs over, the one named last changes fastest.
Arguments:
- query: bfloat16 [1024, 32, 128], P('ctx', 'head'), may hold values from -6 to 6
- key: bfloat16 [1024, 4, 128], P(('ctx', 'head')), may hold values from -6 to 6
- value: bfloat16 [1024, 4, 128], P(('ctx', 'head')), may hold values from -6 to 6
- d_out: bfloat16 [1024, 32, 128], P('ctx', 'head'), may hold values from -6 to 6
- seg_blocks: int32 [4], replicated, may hold values from 1 to 4, 8 in all
- seg_audio: int32 [4], replicated, may hold values 0 or 1
Outputs:
- d_query: bfloat16 [1024, 32, 128], P('ctx', 'head')
- d_key: bfloat16 [1024, 4, 128], P(('ctx', 'head'))
- d_value: bfloat16 [1024, 4, 128], P(('ctx', 'head'))
Inputs may be any that keep to these rules, and one draw needn't show every extreme that they name: `seg_blocks`: the segments tile the 8 blocks in order: their lengths sum to 8.
All inputs are finite; a program needn't handle non-finite values.
Results may differ from a plain program's by a relative error of at most 0.0055.
Values may be sent and summed in bfloat16 or wider, within the bound.
A program may use at most 128 MiB of HBM per device.

v0:
```python
import math

import jax
import jax.numpy as jnp
from jax import lax
from jax.sharding import PartitionSpec as P

DH = 128
GROUP = 8
BLK = 128


NEG = -1e30


def segment_tables(seg_blocks, seg_audio, positions):
    ends = jnp.cumsum(seg_blocks)
    starts = ends - seg_blocks
    blocks = positions // BLK
    inside = (starts[None, :] <= blocks[:, None]) & (blocks[:, None] < ends[None, :])
    numbers = jnp.arange(seg_blocks.shape[0], dtype=jnp.int32)
    segment = jnp.sum(jnp.where(inside, numbers[None, :], 0), axis=1)
    audio = jnp.sum(jnp.where(inside, seg_audio[None, :], 0), axis=1)
    return (segment, audio)


def visible(query_pos, key_pos, query_seg, query_audio, key_seg):
    causal = key_pos[None, :] <= query_pos[:, None]
    span = (query_seg[:, None] == key_seg[None, :]) & (query_audio[:, None] == 1)
    return causal | span


def prepare(rows_query, rows_out, query_pos, seg_blocks, seg_audio):
    tokens = rows_query.shape[0]
    query_seg, query_audio = segment_tables(seg_blocks, seg_audio, query_pos)
    query_flat = rows_query.reshape(tokens * GROUP, DH)
    out_flat = rows_out.reshape(tokens * GROUP, DH)
    return (query_flat, out_flat, query_pos, query_seg, query_audio)


def piece_mask(group_data, keys, seg_blocks, seg_audio):
    query_flat, out_flat, query_pos, query_seg, query_audio = group_data
    key_pos = jnp.arange(keys.shape[0], dtype=jnp.int32)
    key_seg = segment_tables(seg_blocks, seg_audio, key_pos)[0]
    return visible(query_pos, key_pos, query_seg, query_audio, key_seg)


def contract_rows(left, right):
    return lax.dot_general(
        left, right, (((1,), (1,)), ((), ())), preferred_element_type=jnp.float32
    )


def contract_first(left, right):
    return lax.dot_general(
        left, right, (((0,), (0,)), ((), ())), preferred_element_type=jnp.float32
    )


def stats_group(group_data, state, piece, seg_blocks, seg_audio):
    query_flat, out_flat, query_pos, query_seg, query_audio = group_data
    keys, values = piece
    count = keys.shape[0]
    tokens = query_pos.shape[0]
    scale = 1.0 / math.sqrt(DH)
    mask = piece_mask(group_data, keys, seg_blocks, seg_audio)

    def stats_compute(kept):
        highest, total, weighted = kept
        wide = mask[:, None, :]
        scores = (contract_rows(query_flat, keys) * scale).reshape(tokens, GROUP, count)
        new_high = jnp.maximum(highest, jnp.max(jnp.where(wide, scores, NEG), axis=2))
        probs = jnp.where(wide, jnp.exp(scores - new_high[:, :, None]), 0.0)
        d_probs = contract_rows(out_flat, values).reshape(tokens, GROUP, count)
        return (new_high, jnp.sum(probs, axis=2), jnp.sum(probs * d_probs, axis=2))

    def stats_skipped(kept):
        return kept

    return lax.cond(jnp.any(mask), stats_compute, stats_skipped, state)


def grad_group(group_data, finals, grad_rows, piece, seg_blocks, seg_audio):
    query_flat, out_flat, query_pos, query_seg, query_audio = group_data
    lse, delta = finals
    keys, values = piece
    count = keys.shape[0]
    tokens = query_pos.shape[0]
    scale = 1.0 / math.sqrt(DH)
    mask = piece_mask(group_data, keys, seg_blocks, seg_audio)

    def grad_compute(grad_rows):
        wide = mask[:, None, :]
        scores = (contract_rows(query_flat, keys) * scale).reshape(tokens, GROUP, count)
        probs = jnp.where(wide, jnp.exp(scores - lse[:, :, None]), 0.0)
        d_probs = contract_rows(out_flat, values).reshape(tokens, GROUP, count)
        probs_low = probs.astype(jnp.bfloat16).reshape(tokens * GROUP, count)
        d_scores = (
            (probs * (d_probs - delta[:, :, None]))
            .astype(jnp.bfloat16)
            .reshape(tokens * GROUP, count)
        )
        value_part = contract_first(probs_low, out_flat)
        key_part = contract_first(d_scores, query_flat)
        grad_rows = jnp.dot(d_scores, keys, preferred_element_type=jnp.float32)
        return (grad_rows, key_part, value_part)

    def grad_skipped(grad_rows):
        blank = jnp.zeros((count, keys.shape[1]), jnp.float32)
        return (grad_rows, blank, blank)

    return lax.cond(jnp.any(mask), grad_compute, grad_skipped, grad_rows)


def body(query, key, value, d_out, seg_blocks, seg_audio):
    key, value = (
        lax.all_to_all(key, "head", split_axis=1, concat_axis=0, tiled=True),
        lax.all_to_all(value, "head", split_axis=1, concat_axis=0, tiled=True),
    )
    rows = query.shape[0]
    half = rows // 2
    place = lax.axis_index("ctx")
    scale = 1.0 / math.sqrt(DH)
    keys = key[:, 0, :]
    values = value[:, 0, :]
    own_pos = place * rows + jnp.arange(rows, dtype=jnp.int32)
    first = prepare(query[:half], d_out[:half], own_pos[:half], seg_blocks, seg_audio)
    second = prepare(query[half:], d_out[half:], own_pos[half:], seg_blocks, seg_audio)
    groups = (first, second)
    blank_stats = jnp.zeros((half, GROUP), jnp.float32)
    start_stats = tuple(
        (
            (jnp.full((half, GROUP), NEG, jnp.float32), blank_stats, blank_stats)
            for group_data in groups
        )
    )
    piece = (
        lax.all_gather(keys, "ctx", axis=0, tiled=True),
        lax.all_gather(values, "ctx", axis=0, tiled=True),
    )
    stats = tuple(
        (
            stats_group(group_data, state, piece, seg_blocks, seg_audio)
            for group_data, state in zip(groups, start_stats)
        )
    )
    finals = tuple(
        ((highest + jnp.log(total), weighted / total) for highest, total, weighted in stats)
    )
    blank_rows = jnp.zeros((half * GROUP, DH), jnp.float32)
    piece = (
        lax.all_gather(keys, "ctx", axis=0, tiled=True),
        lax.all_gather(values, "ctx", axis=0, tiled=True),
    )
    grad_list = (blank_rows, blank_rows)
    piece_keys = piece[0]
    count = piece_keys.shape[0]
    key_sum = jnp.zeros((count, DH), jnp.float32)
    value_sum = jnp.zeros((count, DH), jnp.float32)
    new_rows = []
    for group_data, group_finals, grad_rows in zip(groups, finals, grad_list):
        grad_rows, key_part, value_part = grad_group(
            group_data, group_finals, grad_rows, piece, seg_blocks, seg_audio
        )
        key_sum = key_sum + key_part
        value_sum = value_sum + value_part
        new_rows.append(grad_rows)
    update = jnp.stack([key_sum, value_sum], axis=1)
    key_grad = update
    grads = (key_grad, tuple(new_rows))
    key_grad, grad_list = grads
    summed = lax.psum_scatter(key_grad, "ctx", scatter_dimension=0, tiled=True)
    d_key = (summed[:, 0, :] * scale).astype(jnp.bfloat16)[:, None, :]
    d_value = summed[:, 1, :].astype(jnp.bfloat16)[:, None, :]
    first_rows = (grad_list[0] * scale).astype(jnp.bfloat16).reshape(half, GROUP, DH)
    second_rows = (grad_list[1] * scale).astype(jnp.bfloat16).reshape(half, GROUP, DH)
    d_query = jnp.concatenate([first_rows, second_rows], axis=0)
    d_key, d_value = (
        lax.all_to_all(d_key, "head", split_axis=0, concat_axis=1, tiled=True),
        lax.all_to_all(d_value, "head", split_axis=0, concat_axis=1, tiled=True),
    )
    return (d_query, d_key, d_value)


def solution(mesh):
    placed = (
        P("ctx", "head", None),
        P(("ctx", "head"), None, None),
        P(("ctx", "head"), None, None),
        P("ctx", "head", None),
        P(),
        P(),
    )
    return jax.shard_map(
        body,
        mesh=mesh,
        in_specs=placed,
        out_specs=(
            P("ctx", "head", None),
            P(("ctx", "head"), None, None),
            P(("ctx", "head"), None, None),
        ),
        check_vma=False,
    )
```

profile of v0, /device:TPU:0, one launch (start us, length us, event | category | flops | bytes accessed | tf_op | source)
XLA Modules:
  0.0 202.9 jit_solution(214252740186446096)
XLA Ops:
  7.2 1.4 copy.30
  8.5 4.2 %all-to-all-start.1 = ((bf16[32,4,128]{2,0,1:T(8,128)(2,1)}), bf16[32,4,128]{2,0,1:T(8,128)(2,1)S(1)}, u32[]{:S(2)}, u32[]{:S(2)}) async-start(bf16[32,4,128]{2,0,1:T(8,128)(2,1)} %copy.30), calls=%async_computation.1 | async-start | bytes 65536 | tf_op jit(solution)/shard_map/all_to_all | solution.py:118
  12.8 0.8 reduce-window.8
  15.2 1.1 slice_bitcast_fusion.2
  16.4 0.9 fusion.16
  17.2 1.4 copy.29
  19.8 3.3 %all-to-all-start = ((bf16[32,4,128]{2,0,1:T(8,128)(2,1)}), bf16[32,4,128]{2,0,1:T(8,128)(2,1)S(1)}, u32[]{:S(2)}, u32[]{:S(2)}) async-start(bf16[32,4,128]{2,0,1:T(8,128)(2,1)} %copy.29), calls=%async_computation | async-start | bytes 65536 | tf_op jit(solution)/shard_map/all_to_all | solution.py:117
  23.2 31.8 %all_gather.9 = bf16[1024,128]{1,0:T(8,128)(2,1)S(1)} all-gather(bf16[128,128]{1,0:T(8,128)(2,1)S(1)} %bitcast.88), channel_id=1, replica_groups=mesh['ctx'=8,'head'=4] {'ctx'}, dimensions={0}, use_global_device_ids=true | all-gather | bytes 294912 | tf_op jit(solution)/shard_map/all_gather | solution.py:139
  54.9 30.7 %all_gather.8 = bf16[1024,128]{1,0:T(8,128)(2,1)S(1)} all-gather(bf16[128,128]{1,0:T(8,128)(2,1)S(1)} %bitcast.89), channel_id=1, replica_groups=mesh['ctx'=8,'head'=4] {'ctx'}, dimensions={0}, use_global_device_ids=true | all-gather | bytes 294912 | tf_op jit(solution)/shard_map/all_gather | solution.py:152
  85.7 2.6 %conditional.4 = (f32[64,8]{1,0:T(8,128)S(1)}, f32[64,8]{1,0:T(8,128)S(1)}, f32[64,8]{1,0:T(8,128)S(1)}) conditional(s32[]{:T(128)} %convert_element_type.36, () %tuple.57, (pred[64,1024]{1,0:T(8,128)(4,1)S(1)}, bf16[512,128]{1,0:T(8,128)(2,1)S(1)}, bf16[1024,128]{1,0:T(8,128)(2,1)S(1)}, bf16[512,128]{1,0:T(8,128)(2,1)S(1)}, ...), branch_computations={%region_5.6_spmd, %region_6.10_spmd} | conditional | flops 274726400 | bytes 7309336 | solution.py:80
  86.4 0.9 multiply_reduce_fusion
  88.3 2.7 %conditional.5 = (f32[512,128]{1,0:T(8,128)S(1)}, f32[1024,128]{1,0:T(8,128)S(1)}, f32[1024,128]{1,0:T(8,128)S(1)}) conditional(s32[]{:T(128)} %convert_element_type.36, () %tuple.56, (pred[64,1024]{1,0:T(8,128)(4,1)S(1)}, bf16[512,128]{1,0:T(8,128)(2,1)S(1)}, bf16[1024,128]{1,0:T(8,128)(2,1)S(1)}, f32[64,8]{1,0:T(8,128)S(1)}, ...), branch_computations={%region_10.11_spmd, %region_11.12_spmd} | conditional | flops 674759168 | bytes 12142616 | solution.py:112
  91.0 2.6 %conditional.6 = (f32[64,8]{1,0:T(8,128)S(1)}, f32[64,8]{1,0:T(8,128)S(1)}, f32[64,8]{1,0:T(8,128)S(1)}) conditional(s32[]{:T(128)} %convert_element_type.38, () %tuple.61, (pred[64,1024]{1,0:T(8,128)(4,1)S(1)}, bf16[512,128]{1,0:T(8,128)(2,1)S(1)}, bf16[1024,128]{1,0:T(8,128)(2,1)S(1)}, bf16[512,128]{1,0:T(8,128)(2,1)S(1)}, ...), branch_computations={%region_15.16_spmd, %region_16.20_spmd} | conditional | flops 274726400 | bytes 7309336 | solution.py:80
  91.8 0.9 multiply_reduce_fusion.1
  93.7 2.7 %conditional.7 = (f32[512,128]{1,0:T(8,128)S(1)}, f32[1024,128]{1,0:T(8,128)S(1)}, f32[1024,128]{1,0:T(8,128)S(1)}) conditional(s32[]{:T(128)} %convert_element_type.38, () %tuple.60, (pred[64,1024]{1,0:T(8,128)(4,1)S(1)}, bf16[512,128]{1,0:T(8,128)(2,1)S(1)}, bf16[1024,128]{1,0:T(8,128)(2,1)S(1)}, f32[64,8]{1,0:T(8,128)S(1)}, ...), branch_computations={%region_20.21_spmd, %region_21.22_spmd} | conditional | flops 674759168 | bytes 12142616 | solution.py:112
  96.6 2.0 pad_maximum_fusion
  99.9 78.2 %all-reduce.3.cloned.1.call-done = f32[1024,2,128]{2,1,0:T(2,128)} async-done(((f32[1024,2,128]{2,1,0:T(2,128)}), f32[1024,2,128]{2,1,0:T(2,128)}) %all-reduce.3.cloned.1.call-update) | async-done | bytes 1048592
  178.1 1.0 dynamic-slice_convert_fusion
  181.0 3.3 %all-to-all-start.3 = ((bf16[4,2,2048]{2,1,0:T(2,128)(2,1)}), bf16[4,2,2048]{2,1,0:T(2,128)(2,1)S(1)}, u32[]{:S(2)}, u32[]{:S(2)}) async-start(bf16[4,2,2048]{2,1,0:T(2,128)(2,1)} %reshape.174), calls=%async_computation.3 | async-start | bytes 65536 | tf_op jit(solution)/shard_map/all_to_all | solution.py:180
  184.3 1.0 fusion.12
  185.3 0.8 reduce.12
  186.7 1.5 all-to-all-done.3
  188.2 3.3 %all-to-all-start.2 = ((bf16[4,2,2048]{2,1,0:T(2,128)(2,1)}), bf16[4,2,2048]{2,1,0:T(2,128)(2,1)S(1)}, u32[]{:S(2)}, u32[]{:S(2)}) async-start(bf16[4,2,2048]{2,1,0:T(2,128)(2,1)} %reshape.172), calls=%async_computation.2 | async-start | bytes 65536 | tf_op jit(solution)/shard_map/all_to_all | solution.py:179
  192.9 2.5 %all-to-all-done.2 = bf16[4,2,2048]{2,1,0:T(2,128)(2,1)S(1)} async-done(((bf16[4,2,2048]{2,1,0:T(2,128)(2,1)}), bf16[4,2,2048]{2,1,0:T(2,128)(2,1)S(1)}, u32[]{:S(2)}, u32[]{:S(2)}) %all-to-all-start.2) | async-done | bytes 32800 | tf_op jit(solution)/shard_map/all_to_all | solution.py:179
  (60 shorter events, 15.9 us)
Async XLA Ops:
  8.5 11.3 %all-to-all-start.1 = ((bf16[32,4,128]{2,0,1:T(8,128)(2,1)}), bf16[32,4,128]{2,0,1:T(8,128)(2,1)S(1)}, u32[]{:S(2)}, u32[]{:S(2)}) async-start(bf16[32,4,128]{2,0,1:T(8,128)(2,1)} %copy.30), calls=%async_computation.1 | async-start | bytes 65536 | tf_op jit(solution)/shard_map/all_to_all | solution.py:118
  19.8 35.1 %all-to-all-start = ((bf16[32,4,128]{2,0,1:T(8,128)(2,1)}), bf16[32,4,128]{2,0,1:T(8,128)(2,1)S(1)}, u32[]{:S(2)}, u32[]{:S(2)}) async-start(bf16[32,4,128]{2,0,1:T(8,128)(2,1)} %copy.29), calls=%async_computation | async-start | bytes 65536 | tf_op jit(solution)/shard_map/all_to_all | solution.py:117
  23.1 154.9 %all-reduce.3.cloned.1.call-start = ((), (), s32[]{:S(2)}) async-start(), calls=%async_computation.4 | async-start | bytes 2097152
  96.5 2.1 %copy-start = (u32[32]{0:T(128)S(1)}, u32[32]{0:T(128)}, u32[]{:S(2)}) copy-start(u32[32]{0:T(128)} %constant.126) | copy-start | bytes 388
  181.0 7.2 %all-to-all-start.3 = ((bf16[4,2,2048]{2,1,0:T(2,128)(2,1)}), bf16[4,2,2048]{2,1,0:T(2,128)(2,1)S(1)}, u32[]{:S(2)}, u32[]{:S(2)}) async-start(bf16[4,2,2048]{2,1,0:T(2,128)(2,1)} %reshape.174), calls=%async_computation.3 | async-start | bytes 65536 | tf_op jit(solution)/shard_map/all_to_all | solution.py:180
  188.2 7.2 %all-to-all-start.2 = ((bf16[4,2,2048]{2,1,0:T(2,128)(2,1)}), bf16[4,2,2048]{2,1,0:T(2,128)(2,1)S(1)}, u32[]{:S(2)}, u32[]{:S(2)}) async-start(bf16[4,2,2048]{2,1,0:T(2,128)(2,1)} %reshape.172), calls=%async_computation.2 | async-start | bytes 65536 | tf_op jit(solution)/shard_map/all_to_all | solution.py:179
Sparse Core Ops, SparseCore 0:
  98.7 79.3 all-reduce.2
where the time goes:
time: 204 us; the launch traced here: 203 us
  waiting for transfers between devices  82.2 us (40%)
  blocking collectives  62.5 us (31%)
  between operations  16 us (8%)
  starting transfers between devices  14.1 us (7%)
  other arithmetic  10.4 us (5%)
  local copies, waits for them, and re-layouts  9.44 us (5%)
  matrix products  8.14 us (4%)
    unnamed x2, waiting for transfers between devices  78.2 us
    all_gather x1, blocking collectives, body(): lax.all_gather(values, 'ctx', axis=0, tiled=True)  31.8 us
    all_gather x1, blocking collectives, body(): lax.all_gather(keys, 'ctx', axis=0, tiled=True)  30.7 us
    unnamed x13, local copies, waits for them, and re-layouts  5.96 us
    dot_general x8, matrix products, contract_rows(): lax.dot_general(left, right, (((1,), (1,)), ((), ())), preferred_element_...  5.37 us
    all_to_all x1, starting transfers between devices, body(): lax.all_to_all(value, 'head', split_axis=1, concat_axis=0, tiled=True)  4.21 us
  transfers between devices with their start and end apart: 5, of which 3 were waited for; matrix products, arithmetic and copies ran while one was open for 5% of the time, Pallas kernels for 0%

commit v1 on v0

--- a/solution.py
+++ b/solution.py
@@ -1,9 +1,16 @@
+import functools
 import math
 
 import jax
 import jax.numpy as jnp
 from jax import lax
+from jax.experimental import pallas as pl
+from jax.experimental.pallas import tpu as pltpu
 from jax.sharding import PartitionSpec as P
+
+MESH = pl.DeviceIdType.MESH
+VMEM_BUDGET = 48 * 2**20
+ROW_CHUNK = 256
 
 DH = 128
 GROUP = 8
@@ -182,6 +189,268 @@
     return (d_query, d_key, d_value)
 
 
+def fused_kernel(
+    n, heads, q_ref, do_ref, k_ref, v_ref, blocks_ref, audio_ref,
+    dq_ref, dk_ref, dv_ref,
+    head_out, kv, p_s, dp_s, ds_s, m_s, l_s, w_s, own_part,
+    gy_out, gy_in, gz_out, gz_in, fin_out, fin_in,
+    h_send, h_recv, kv_recv, kvz_send, kvy_send,
+    gy_send, gy_recv, gz_send, gz_recv, f_send, f_recv,
+):
+    chain = n // 2
+    place = lax.axis_index("ctx")
+    head = lax.axis_index("head")
+    a, b = place // 2, lax.rem(place, 2)
+    rows_flat = q_ref.shape[0]
+    rows = rows_flat // GROUP
+    part = rows // heads
+    scale = 1.0 / math.sqrt(DH)
+    power = scale * math.log2(math.e)
+    chunk = min(ROW_CHUNK, rows_flat)
+    chunks = [slice(r, r + chunk) for r in range(0, rows_flat, chunk)]
+
+    def head_peer(d):
+        return lax.rem(head + d, heads)
+
+    def up(d):
+        return lax.rem(a + d, chain)
+
+    def down(d):
+        return lax.rem(a + chain - d, chain)
+
+    def at(ctx_index, head_index):
+        return (ctx_index, head_index)
+
+    partner = 2 * a + 1 - b
+
+    def send(src, dst, send_sem, recv_sem, target):
+        return pltpu.make_async_remote_copy(
+            src_ref=src, dst_ref=dst, send_sem=send_sem, recv_sem=recv_sem,
+            device_id=target, device_id_type=MESH,
+        )
+
+    barrier = pltpu.get_barrier_semaphore()
+    for d in range(1, heads):
+        pl.semaphore_signal(barrier, inc=1, device_id=at(place, head_peer(d)), device_id_type=MESH)
+    pl.semaphore_signal(barrier, inc=1, device_id=at(partner, head), device_id_type=MESH)
+    for d in range(1, chain):
+        pl.semaphore_signal(barrier, inc=1, device_id=at(2 * up(d) + b, head), device_id_type=MESH)
+
+    for i in range(heads):
+        head_out[i, 0] = k_ref[:, i, :]
+        head_out[i, 1] = v_ref[:, i, :]
+    pl.semaphore_wait(barrier, heads - 1 + chain)
+
+    mine = pl.ds(pl.multiple_of(head * part, part), part)
+
+    def head_copy(d):
+        peer = head_peer(d)
+        return send(head_out.at[peer], kv.at[place, :, mine, :], h_send.at[d], h_recv.at[d], at(place, peer))
+
+    for d in range(1, heads):
+        head_copy(d).start()
+    kv[place, :, mine, :] = head_out[head]
+
+    pos = place * rows + lax.broadcasted_iota(jnp.int32, (1, rows_flat), 1) // GROUP
+    limit = pos + 1
+    start = jnp.int32(0)
+    for s in range(blocks_ref.shape[0]):
+        end = start + blocks_ref[s] * BLK
+        inside = (pos >= start) & (pos < end) & (jnp.broadcast_to(audio_ref[s], pos.shape) == 1)
+        limit = jnp.where(inside, end, limit)
+        start = end
+
+    for d in range(1, heads):
+        head_copy(d).wait_recv()
+
+    def chain_copy(d):
+        return send(kv.at[place], kv.at[place], kvz_send.at[d], kv_recv.at[place], at(2 * up(d) + b, head))
+
+    def relay_copy(d):
+        slot = 2 * down(d) + b
+        return send(kv.at[slot], kv.at[slot], kvy_send.at[d], kv_recv.at[slot], at(partner, head))
+
+    relay_copy(0).start()
+    for d in range(1, chain):
+        chain_copy(d).start()
+
+    def stats_step(t, carry):
+        d = t // 2
+        own_column = lax.rem(t, 2) == 0
+        slot = 2 * down(d) + lax.rem(b + t, 2)
+
+        @pl.when(t > 0)
+        def _():
+            send(kv.at[slot], kv.at[slot], kvy_send.at[d], kv_recv.at[slot], at(partner, head)).wait_recv()
+
+        @pl.when(own_column & (t > 0))
+        def _():
+            relay_copy(d).start()
+
+        keys, values = kv[slot, 0], kv[slot, 1]
+        key_pos = slot * rows + lax.broadcasted_iota(jnp.int32, (rows, 1), 0)
+        for c in chunks:
+            s = contract_rows(keys, q_ref[c, :])
+            s = jnp.where(key_pos < limit[:, c], s, NEG)
+            high = jnp.max(s, axis=0, keepdims=True)
+            p = jnp.exp2((s - high) * power)
+            dp = contract_rows(values, do_ref[c, :])
+            p_s[slot, :, c] = p
+            dp_s[slot, :, c] = dp
+            m_s[slot, :, c] = high
+            l_s[slot, :, c] = jnp.sum(p, axis=0, keepdims=True)
+            w_s[slot, :, c] = jnp.sum(p * dp, axis=0, keepdims=True)
+        return carry
+
+    lax.fori_loop(0, n, stats_step, 0)
+
+    m_all = m_s[...]
+    high = jnp.max(m_all, axis=0)
+    factors = jnp.exp2((m_all - high[None]) * power)
+    total = jnp.sum(factors * l_s[...], axis=0)
+    delta = jnp.sum(factors * w_s[...], axis=0) / total
+    m_s[...] = factors / total[None]
+
+    def pair_copy(d):
+        dest = down(d)
+        return send(gy_out.at[d], gy_in.at[dest], gy_send.at[d], gy_recv.at[dest], at(partner, head))
+
+    def sum_copy(d):
+        return send(gz_out.at[d], gz_in.at[a], gz_send.at[d], gz_recv.at[a], at(2 * down(d) + b, head))
+
+    def combine(d):
+        pair_copy(d).wait_recv()
+        return own_part[d] + gy_in[down(d)].astype(jnp.float32)
+
+    def grad_step(t, carry):
+        d = lax.rem(t // 2 + 1, chain)
+        other_column = lax.rem(t, 2) == 0
+        slot = 2 * down(d) + lax.rem(b + t + 1, 2)
+        key_part = jnp.zeros((rows, DH), jnp.float32)
+        value_part = jnp.zeros((rows, DH), jnp.float32)
+        for c in chunks:
+            probs = p_s[slot, :, c] * m_s[slot, :, c]
+            ds = (probs * (dp_s[slot, :, c] - delta[:, c])).astype(jnp.bfloat16)
+            ds_s[slot, :, c] = ds
+            value_part += jnp.dot(probs.astype(jnp.bfloat16), do_ref[c, :], preferred_element_type=jnp.float32)
+            key_part += jnp.dot(ds, q_ref[c, :], preferred_element_type=jnp.float32)
+
+        @pl.when(other_column)
+        def _():
+            gy_out[d, 0] = key_part.astype(jnp.bfloat16)
+            gy_out[d, 1] = value_part.astype(jnp.bfloat16)
+            pair_copy(d).start()
+
+        @pl.when(jnp.logical_not(other_column))
+        def _():
+            own_part[d, 0] = key_part
+            own_part[d, 1] = value_part
+
+        @pl.when(jnp.logical_not(other_column) & (t > 1))
+        def _():
+            before = t // 2
+            gz_out[before] = combine(before).astype(jnp.bfloat16)
+            sum_copy(before).start()
+
+        return carry
+
+    lax.fori_loop(0, n, grad_step, 0)
+
+    all_keys = kv[:, 0].reshape(n * rows, DH)
+    all_ds = ds_s[...].reshape(n * rows, rows_flat)
+    dq = contract_first(all_keys, all_ds) * scale
+    dq_ref[...] = dq.T.astype(jnp.bfloat16)
+
+    acc = combine(0)
+    for d in range(1, chain):
+        source = up(d)
+        send(gz_out.at[d], gz_in.at[source], gz_send.at[d], gz_recv.at[source], at(2 * down(d) + b, head)).wait_recv()
+        acc = acc + gz_in[source].astype(jnp.float32)
+    fin_out[0] = (acc[0] * scale).astype(jnp.bfloat16)
+    fin_out[1] = acc[1].astype(jnp.bfloat16)
+
+    def final_copy(d):
+        peer = head_peer(d)
+        theirs = pl.ds(pl.multiple_of(peer * part, part), part)
+        return send(fin_out.at[:, theirs, :], fin_in.at[head], f_send.at[d], f_recv.at[d], at(place, peer))
+
+    for d in range(1, heads):
+        final_copy(d).start()
+    fin_in[head] = fin_out[:, mine, :]
+    for d in range(1, heads):
+        final_copy(d).wait_recv()
+    for i in range(heads):
+        dk_ref[:, i, :] = fin_in[i, 0]
+        dv_ref[:, i, :] = fin_in[i, 1]
+
+    for d in range(1, heads):
+        head_copy(d).wait_send()
+        final_copy(d).wait_send()
+    for d in range(chain):
+        relay_copy(d).wait_send()
+        pair_copy(d).wait_send()
+    for d in range(1, chain):
+        chain_copy(d).wait_send()
+        sum_copy(d).wait_send()
+
+
+def fused_scratch(n, heads, rows):
+    flat, chain, part = rows * GROUP, n // 2, rows // heads
+    low, full, sem = jnp.bfloat16, jnp.float32, pltpu.SemaphoreType.DMA
+    return [
+        pltpu.VMEM((heads, 2, part, DH), low),
+        pltpu.VMEM((n, 2, rows, DH), low),
+        pltpu.VMEM((n, rows, flat), full),
+        pltpu.VMEM((n, rows, flat), full),
+        pltpu.VMEM((n, rows, flat), low),
+        pltpu.VMEM((n, 1, flat), full),
+        pltpu.VMEM((n, 1, flat), full),
+        pltpu.VMEM((n, 1, flat), full),
+        pltpu.VMEM((chain, 2, rows, DH), full),
+        pltpu.VMEM((chain, 2, rows, DH), low),
+        pltpu.VMEM((chain, 2, rows, DH), low),
+        pltpu.VMEM((chain, 2, rows, DH), low),
+        pltpu.VMEM((chain, 2, rows, DH), low),
+        pltpu.VMEM((2, rows, DH), low),
+        pltpu.VMEM((heads, 2, part, DH), low),
+        sem((heads,)), sem((heads,)), sem((n,)), sem((chain,)), sem((chain,)),
+        sem((chain,)), sem((chain,)), sem((chain,)), sem((chain,)), sem((heads,)), sem((heads,)),
+    ]
+
+
+def fused_body(n, heads, query, key, value, d_out, seg_blocks, seg_audio):
+    rows = query.shape[0]
+    flat = rows * GROUP
+    low = jnp.bfloat16
+    vmem, smem = pl.BlockSpec(memory_space=pltpu.VMEM), pl.BlockSpec(memory_space=pltpu.SMEM)
+    d_query, d_key, d_value = pl.pallas_call(
+        functools.partial(fused_kernel, n, heads),
+        out_shape=[
+            jax.ShapeDtypeStruct((flat, DH), low),
+            jax.ShapeDtypeStruct(key.shape, low),
+            jax.ShapeDtypeStruct(value.shape, low),
+        ],
+        in_specs=[vmem] * 4 + [smem] * 2,
+        out_specs=[vmem] * 3,
+        scratch_shapes=fused_scratch(n, heads, rows),
+        cost_estimate=pl.CostEstimate(
+            flops=10 * n * rows * flat * DH, bytes_accessed=6 * flat * DH, transcendentals=n * rows * flat
+        ),
+        compiler_params=pltpu.CompilerParams(
+            collective_id=0, has_side_effects=True, vmem_limit_bytes=VMEM_BUDGET
+        ),
+    )(query.reshape(flat, DH), d_out.reshape(flat, DH), key, value, seg_blocks, seg_audio)
+    return d_query.reshape(query.shape), d_key, d_value
+
+
+def plan_body(n, heads, query, key, value, d_out, seg_blocks, seg_audio):
+    rows = query.shape[0]
+    held = n * rows * rows * GROUP * 10
+    if held > VMEM_BUDGET // 2 or n % 2 or query.shape[1] != GROUP or key.shape[1] != heads:
+        return body(query, key, value, d_out, seg_blocks, seg_audio)
+    return fused_body(n, heads, query, key, value, d_out, seg_blocks, seg_audio)
+
+
 def solution(mesh):
     placed = (
         P("ctx", "head", None),
@@ -192,7 +461,7 @@
         P(),
     )
     return jax.shard_map(
-        body,
+        functools.partial(plan_body, mesh.shape["ctx"], mesh.shape["head"]),
         mesh=mesh,
         in_specs=placed,
         out_specs=(

time: 204 us -> 45.7 us (0.22)
  waiting for transfers between devices: 82.2 us -> 0 us
  blocking collectives: 62.5 us -> 0 us
  Pallas kernels: 0 us -> 38.7 us
  between operations: 16 us -> 0.66 us
  starting transfers between devices: 14.1 us -> 0 us
  other arithmetic: 10.4 us -> 0 us
  matrix products: 8.14 us -> 0 us
  local copies, waits for them, and re-layouts: 9.44 us -> 6 us
    unnamed x2 -> x0, waiting for transfers between devices: 78.2 us -> none
    all_gather x2 -> x0, blocking collectives: 62.5 us -> none  [the longest x1 31.8 us: body(): lax.all_gather(values, 'ctx', axis=0, tiled=True)]
    pallas_call x0 -> x1, Pallas kernels: none -> 38.7 us  [fused_body(): pl.pallas_call(functools.partial(fused_kernel, n, heads), out_shape=[jax....]
    all_to_all x4 -> x0, starting transfers between devices: 14 us -> none  [the longest x1 4.21 us: body(): lax.all_to_all(value, 'head', split_axis=1, concat_axis=0, tiled=True)]
    dot_general x14 -> x0, matrix products: 8.14 us -> none  [the longest x8 5.37 us: contract_rows(): lax.dot_general(left, right, (((1,), (1,)), ((), ())), preferred_element_...]
    all_to_all x4 -> x0, waiting for transfers between devices: 3.97 us -> none  [the longest x1 2.5 us: body(): lax.all_to_all(d_key, 'head', split_axis=0, concat_axis=1, tiled=True)]
    another operation x5 -> x0, other arithmetic: 3.64 us -> none  [the longest x1 1.98 us: body(): update = jnp.stack([key_sum, value_sum], axis=1)]
    reduce_sum x4 -> x0, other arithmetic: 2.35 us -> none  [the longest x2 1.52 us: stats_compute(): return (new_high, jnp.sum(probs, axis=2), jnp.sum(probs * d_probs, axis=2))]
  transfers between devices with their start and end apart: 5 -> 0, of which waited for: 3 -> 0; matrix products, arithmetic and copies ran while one was open for 5% -> 0% of each run, Pallas kernels for 0% -> 0%
where the time goes in v1:
time: 45.7 us; the launch traced here: 45.4 us
  Pallas kernels  38.7 us (85%)
  local copies, waits for them, and re-layouts  6 us (13%)
  between operations  0.66 us (1%)
    pallas_call x1, Pallas kernels, fused_body(): pl.pallas_call(functools.partial(fused_kernel, n, heads), out_shape=[jax....  38.7 us
    unnamed x15, local copies, waits for them, and re-layouts  6 us

profile of v1, /device:TPU:0, one launch (start us, length us, event | category | flops | bytes accessed | tf_op | source)
XLA Modules:
  0.0 45.4 jit_solution(295285724744909082)
XLA Ops:
  0.6 0.0 copy-start.4
  0.6 0.0 copy-start.5
  0.7 0.6 %copy-done.4 = s32[4]{0:T(128)S(1)} copy-done((s32[4]{0:T(128)S(1)}, s32[4]{0:T(128)}, u32[]{:S(2)}) %copy-start.4) | copy-done | bytes 40
  1.3 0.0 copy-done.5
  1.3 0.0 copy-start
  1.3 0.9 %copy-done = bf16[128,8,128]{2,1,0:T(8,128)(2,1)S(1)} copy-done((bf16[128,8,128]{2,1,0:T(8,128)(2,1)S(1)}, bf16[128,8,128]{2,1,0:T(8,128)(2,1)}, u32[]{:S(2)}) %copy-start) | copy-done | bytes 262168
  2.3 0.0 copy-start.1
  2.3 0.9 %copy-done.1 = bf16[128,8,128]{2,1,0:T(8,128)(2,1)S(1)} copy-done((bf16[128,8,128]{2,1,0:T(8,128)(2,1)S(1)}, bf16[128,8,128]{2,1,0:T(8,128)(2,1)}, u32[]{:S(2)}) %copy-start.1) | copy-done | bytes 262168
  3.2 0.0 copy-start.2
  3.2 0.8 %copy-done.2 = bf16[32,4,128]{2,1,0:T(4,128)(2,1)S(1)} copy-done((bf16[32,4,128]{2,1,0:T(4,128)(2,1)S(1)}, bf16[32,4,128]{2,1,0:T(4,128)(2,1)}, u32[]{:S(2)}) %copy-start.2) | copy-done | bytes 32792
  4.0 0.0 copy-start.3
  4.0 0.8 %copy-done.3 = bf16[32,4,128]{2,1,0:T(4,128)(2,1)S(1)} copy-done((bf16[32,4,128]{2,1,0:T(4,128)(2,1)S(1)}, bf16[32,4,128]{2,1,0:T(4,128)(2,1)}, u32[]{:S(2)}) %copy-start.3) | copy-done | bytes 32792
  4.7 38.7 %shard_map.85 = (bf16[1024,128]{1,0:T(8,128)(2,1)S(1)}, bf16[32,4,128]{2,1,0:T(4,128)(2,1)S(1)}, bf16[32,4,128]{2,1,0:T(4,128)(2,1)S(1)}) custom-call(bf16[1024,128]{1,0:T(8,128)(2,1)S(1)} %bitcast.4, bf16[1024,128]{1,0:T(8,128)(2,1)S(1)} %bitcast.5, bf16[32,4,128]{2,1,0:T(4,128)(2,1)S(1)} %copy-done.2, bf16[32,4,128]{2,1,0:T(4,128)(2,1)S(1)} %copy-done.3, ...), custom_call_target="tpu_custom_call" | custom-call | flops 1342177280 | bytes 786432 | tf_op jit(solution)/shard_map/pallas_call | solution.py:426
  43.5 0.7 %copy.12 = bf16[128,8,128]{2,1,0:T(8,128)(2,1)} copy(bf16[128,8,128]{2,1,0:T(8,128)(2,1)S(1)} %bitcast.3) | data formatting | bytes 524288
  44.2 0.6 %copy.13 = bf16[32,4,128]{2,1,0:T(4,128)(2,1)} copy(bf16[32,4,128]{2,1,0:T(4,128)(2,1)S(1)} %get-tuple-element.13) | data formatting | bytes 65536
  44.8 0.6 %copy.14 = bf16[32,4,128]{2,1,0:T(4,128)(2,1)} copy(bf16[32,4,128]{2,1,0:T(4,128)(2,1)S(1)} %get-tuple-element.14) | data formatting | bytes 65536
Async XLA Ops:
  0.6 0.7 %copy-start.4 = (s32[4]{0:T(128)S(1)}, s32[4]{0:T(128)}, u32[]{:S(2)}) copy-start(s32[4]{0:T(128)} %blocks_ref.1) | copy-start | bytes 52
  0.6 0.7 %copy-start.5 = (s32[4]{0:T(128)S(1)}, s32[4]{0:T(128)}, u32[]{:S(2)}) copy-start(s32[4]{0:T(128)} %audio_ref.1) | copy-start | bytes 52
  1.3 0.9 %copy-start = (bf16[128,8,128]{2,1,0:T(8,128)(2,1)S(1)}, bf16[128,8,128]{2,1,0:T(8,128)(2,1)}, u32[]{:S(2)}) copy-start(bf16[128,8,128]{2,1,0:T(8,128)(2,1)} %param.6) | copy-start | bytes 786436
  2.3 0.9 %copy-start.1 = (bf16[128,8,128]{2,1,0:T(8,128)(2,1)S(1)}, bf16[128,8,128]{2,1,0:T(8,128)(2,1)}, u32[]{:S(2)}) copy-start(bf16[128,8,128]{2,1,0:T(8,128)(2,1)} %param.9) | copy-start | bytes 786436
  3.2 0.8 %copy-start.2 = (bf16[32,4,128]{2,1,0:T(4,128)(2,1)S(1)}, bf16[32,4,128]{2,1,0:T(4,128)(2,1)}, u32[]{:S(2)}) copy-start(bf16[32,4,128]{2,1,0:T(4,128)(2,1)} %k_ref.1) | copy-start | bytes 98308
  4.0 0.8 %copy-start.3 = (bf16[32,4,128]{2,1,0:T(4,128)(2,1)S(1)}, bf16[32,4,128]{2,1,0:T(4,128)(2,1)}, u32[]{:S(2)}) copy-start(bf16[32,4,128]{2,1,0:T(4,128)(2,1)} %v_ref.1) | copy-start | bytes 98308

commit v2 on v1

--- a/solution.py
+++ b/solution.py
@@ -9,7 +9,7 @@
 from jax.sharding import PartitionSpec as P
 
 MESH = pl.DeviceIdType.MESH
-VMEM_BUDGET = 48 * 2**20
+VMEM_BUDGET = 60 * 2**20
 ROW_CHUNK = 256
 
 DH = 128
@@ -190,12 +190,13 @@
 
 
 def fused_kernel(
-    n, heads, q_ref, do_ref, k_ref, v_ref, blocks_ref, audio_ref,
+    n, heads, q_hbm, do_hbm, k_hbm, v_hbm, blocks_hbm, audio_hbm,
     dq_ref, dk_ref, dv_ref,
+    q_ref, do_ref, k_ref, v_ref, blocks_ref, audio_ref, q_turned, do_turned,
     head_out, kv, p_s, dp_s, ds_s, m_s, l_s, w_s, own_part,
-    gy_out, gy_in, gz_out, gz_in, fin_out, fin_in,
-    h_send, h_recv, kv_recv, kvz_send, kvy_send,
-    gy_send, gy_recv, gz_send, gz_recv, f_send, f_recv,
+    gy_out, gy_in, gz_out, gz_in,
+    in_sem, kvz_send, kvz_recv, kvy_send, kvy_recv,
+    gy_send, gy_recv, gz_send, gz_recv,
 ):
     chain = n // 2
     place = lax.axis_index("ctx")
@@ -229,27 +230,65 @@
             device_id=target, device_id_type=MESH,
         )
 
+    pairs = [(da, dh) for da in range(chain) for dh in range(heads)]
+    others = pairs[1:]
+
     barrier = pltpu.get_barrier_semaphore()
-    for d in range(1, heads):
-        pl.semaphore_signal(barrier, inc=1, device_id=at(place, head_peer(d)), device_id_type=MESH)
+    for da, dh in others:
+        pl.semaphore_signal(
+            barrier, inc=1, device_id=at(2 * up(da) + b, head_peer(dh)), device_id_type=MESH
+        )
     pl.semaphore_signal(barrier, inc=1, device_id=at(partner, head), device_id_type=MESH)
-    for d in range(1, chain):
-        pl.semaphore_signal(barrier, inc=1, device_id=at(2 * up(d) + b, head), device_id_type=MESH)
-
+
+    loads = [
+        pltpu.make_async_copy(src, dst, in_sem.at[i])
+        for i, (src, dst) in enumerate((
+            (k_hbm, k_ref), (v_hbm, v_ref), (blocks_hbm, blocks_ref),
+            (audio_hbm, audio_ref), (q_hbm, q_ref), (do_hbm, do_ref),
+        ))
+    ]
+    for load in loads:
+        load.start()
+    loads[0].wait()
+    loads[1].wait()
     for i in range(heads):
         head_out[i, 0] = k_ref[:, i, :]
         head_out[i, 1] = v_ref[:, i, :]
-    pl.semaphore_wait(barrier, heads - 1 + chain)
+    pl.semaphore_wait(barrier, chain * heads)
 
     mine = pl.ds(pl.multiple_of(head * part, part), part)
 
-    def head_copy(d):
-        peer = head_peer(d)
-        return send(head_out.at[peer], kv.at[place, :, mine, :], h_send.at[d], h_recv.at[d], at(place, peer))
-
-    for d in range(1, heads):
-        head_copy(d).start()
+    def chain_copy(da, dh):
+        peer = head_peer(dh)
+        return send(
+            head_out.at[peer], kv.at[place, :, mine, :], kvz_send.at[da * heads + dh],
+            kvz_recv.at[a * heads + head], at(2 * up(da) + b, peer),
+        )
+
+    def chain_arrival(d, dh):
+        source, peer = down(d), head_peer(dh)
+        theirs = pl.ds(pl.multiple_of(peer * part, part), part)
+        return send(
+            head_out.at[peer], kv.at[2 * source + b, :, theirs, :], kvz_send.at[0],
+            kvz_recv.at[source * heads + peer], at(partner, head),
+        )
+
+    def relay_copy(d):
+        slot = 2 * down(d) + b
+        return send(kv.at[slot], kv.at[slot], kvy_send.at[d], kvy_recv.at[down(d)], at(partner, head))
+
+    def relay_arrival(d):
+        slot = 2 * down(d) + 1 - b
+        return send(kv.at[slot], kv.at[slot], kvy_send.at[d], kvy_recv.at[down(d)], at(partner, head))
+
+    for da, dh in others:
+        chain_copy(da, dh).start()
     kv[place, :, mine, :] = head_out[head]
+
+    for load in loads[2:]:
+        load.wait()
+    q_turned[...] = q_ref[...].T
+    do_turned[...] = do_ref[...].T
 
     pos = place * rows + lax.broadcasted_iota(jnp.int32, (1, rows_flat), 1) // GROUP
     limit = pos + 1
@@ -260,41 +299,33 @@
         limit = jnp.where(inside, end, limit)
         start = end
 
-    for d in range(1, heads):
-        head_copy(d).wait_recv()
-
-    def chain_copy(d):
-        return send(kv.at[place], kv.at[place], kvz_send.at[d], kv_recv.at[place], at(2 * up(d) + b, head))
-
-    def relay_copy(d):
-        slot = 2 * down(d) + b
-        return send(kv.at[slot], kv.at[slot], kvy_send.at[d], kv_recv.at[slot], at(partner, head))
-
+    for dh in range(1, heads):
+        chain_arrival(0, dh).wait_recv()
     relay_copy(0).start()
-    for d in range(1, chain):
-        chain_copy(d).start()
 
     def stats_step(t, carry):
         d = t // 2
         own_column = lax.rem(t, 2) == 0
         slot = 2 * down(d) + lax.rem(b + t, 2)
 
-        @pl.when(t > 0)
-        def _():
-            send(kv.at[slot], kv.at[slot], kvy_send.at[d], kv_recv.at[slot], at(partner, head)).wait_recv()
-
         @pl.when(own_column & (t > 0))
         def _():
+            for dh in range(heads):
+                chain_arrival(d, dh).wait_recv()
             relay_copy(d).start()
+
+        @pl.when(jnp.logical_not(own_column))
+        def _():
+            relay_arrival(d).wait_recv()
 
         keys, values = kv[slot, 0], kv[slot, 1]
         key_pos = slot * rows + lax.broadcasted_iota(jnp.int32, (rows, 1), 0)
         for c in chunks:
-            s = contract_rows(keys, q_ref[c, :])
+            s = jnp.dot(keys, q_turned[:, c], preferred_element_type=jnp.float32)
             s = jnp.where(key_pos < limit[:, c], s, NEG)
             high = jnp.max(s, axis=0, keepdims=True)
             p = jnp.exp2((s - high) * power)
-            dp = contract_rows(values, do_ref[c, :])
+            dp = jnp.dot(values, do_turned[:, c], preferred_element_type=jnp.float32)
             p_s[slot, :, c] = p
             dp_s[slot, :, c] = dp
             m_s[slot, :, c] = high
@@ -315,8 +346,19 @@
         dest = down(d)
         return send(gy_out.at[d], gy_in.at[dest], gy_send.at[d], gy_recv.at[dest], at(partner, head))
 
-    def sum_copy(d):
-        return send(gz_out.at[d], gz_in.at[a], gz_send.at[d], gz_recv.at[a], at(2 * down(d) + b, head))
+    def sum_copy(d, dh):
+        peer = head_peer(dh)
+        theirs = pl.ds(pl.multiple_of(peer * part, part), part)
+        return send(
+            gz_out.at[d, :, theirs, :], gz_in.at[a * heads + head], gz_send.at[d * heads + dh],
+            gz_recv.at[a * heads + head], at(2 * down(d) + b, peer),
+        )
+
+    def sum_arrival(da, dh):
+        index = up(da) * heads + head_peer(dh)
+        return send(
+            gz_out.at[0, :, mine, :], gz_in.at[index], gz_send.at[0], gz_recv.at[index], at(partner, head)
+        )
 
     def combine(d):
         pair_copy(d).wait_recv()
@@ -350,54 +392,56 @@
         def _():
             before = t // 2
             gz_out[before] = combine(before).astype(jnp.bfloat16)
-            sum_copy(before).start()
+            for dh in range(heads):
+                sum_copy(before, dh).start()
 
         return carry
 
     lax.fori_loop(0, n, grad_step, 0)
 
     all_keys = kv[:, 0].reshape(n * rows, DH)
-    all_ds = ds_s[...].reshape(n * rows, rows_flat)
-    dq = contract_first(all_keys, all_ds) * scale
-    dq_ref[...] = dq.T.astype(jnp.bfloat16)
-
-    acc = combine(0)
-    for d in range(1, chain):
-        source = up(d)
-        send(gz_out.at[d], gz_in.at[source], gz_send.at[d], gz_recv.at[source], at(2 * down(d) + b, head)).wait_recv()
-        acc = acc + gz_in[source].astype(jnp.float32)
-    fin_out[0] = (acc[0] * scale).astype(jnp.bfloat16)
-    fin_out[1] = acc[1].astype(jnp.bfloat16)
-
-    def final_copy(d):
-        peer = head_peer(d)
-        theirs = pl.ds(pl.multiple_of(peer * part, part), part)
-        return send(fin_out.at[:, theirs, :], fin_in.at[head], f_send.at[d], f_recv.at[d], at(place, peer))
-
-    for d in range(1, heads):
-        final_copy(d).start()
-    fin_in[head] = fin_out[:, mine, :]
-    for d in range(1, heads):
-        final_copy(d).wait_recv()
+
+    def query_rows(c):
+        all_ds = ds_s[:, :, c].reshape(n * rows, c.stop - c.start)
+        dq_ref[c, :] = (contract_first(all_keys, all_ds) * scale).T.astype(jnp.bfloat16)
+
+    middle = rows_flat // 2
+    query_rows(slice(0, middle))
+    gz_out[0] = combine(0).astype(jnp.bfloat16)
+    for dh in range(1, heads):
+        sum_copy(0, dh).start()
+    gz_in[a * heads + head] = gz_out[0, :, mine, :]
+    query_rows(slice(middle, rows_flat))
+
+    for da, dh in others:
+        sum_arrival(da, dh).wait_recv()
     for i in range(heads):
-        dk_ref[:, i, :] = fin_in[i, 0]
-        dv_ref[:, i, :] = fin_in[i, 1]
-
-    for d in range(1, heads):
-        head_copy(d).wait_send()
-        final_copy(d).wait_send()
+        acc = gz_in[i].astype(jnp.float32)
+        for source in range(1, chain):
+            acc = acc + gz_in[source * heads + i].astype(jnp.float32)
+        dk_ref[:, i, :] = (acc[0] * scale).astype(jnp.bfloat16)
+        dv_ref[:, i, :] = acc[1].astype(jnp.bfloat16)
+
+    for da, dh in others:
+        chain_copy(da, dh).wait_send()
+        sum_copy(da, dh).wait_send()
     for d in range(chain):
         relay_copy(d).wait_send()
         pair_copy(d).wait_send()
-    for d in range(1, chain):
-        chain_copy(d).wait_send()
-        sum_copy(d).wait_send()
-
-
-def fused_scratch(n, heads, rows):
+
+
+def fused_scratch(n, heads, rows, segments):
     flat, chain, part = rows * GROUP, n // 2, rows // heads
     low, full, sem = jnp.bfloat16, jnp.float32, pltpu.SemaphoreType.DMA
     return [
+        pltpu.VMEM((flat, DH), low),
+        pltpu.VMEM((flat, DH), low),
+        pltpu.VMEM((part, heads, DH), low),
+        pltpu.VMEM((part, heads, DH), low),
+        pltpu.SMEM((segments,), jnp.int32),
+        pltpu.SMEM((segments,), jnp.int32),
+        pltpu.VMEM((DH, flat), low),
+        pltpu.VMEM((DH, flat), low),
         pltpu.VMEM((heads, 2, part, DH), low),
         pltpu.VMEM((n, 2, rows, DH), low),
         pltpu.VMEM((n, rows, flat), full),
@@ -410,11 +454,9 @@
         pltpu.VMEM((chain, 2, rows, DH), low),
         pltpu.VMEM((chain, 2, rows, DH), low),
         pltpu.VMEM((chain, 2, rows, DH), low),
-        pltpu.VMEM((chain, 2, rows, DH), low),
-        pltpu.VMEM((2, rows, DH), low),
-        pltpu.VMEM((heads, 2, part, DH), low),
-        sem((heads,)), sem((heads,)), sem((n,)), sem((chain,)), sem((chain,)),
-        sem((chain,)), sem((chain,)), sem((chain,)), sem((chain,)), sem((heads,)), sem((heads,)),
+        pltpu.VMEM((chain * heads, 2, part, DH), low),
+        sem((6,)), sem((chain * heads,)), sem((chain * heads,)), sem((chain,)), sem((chain,)),
+        sem((chain,)), sem((chain,)), sem((chain * heads,)), sem((chain * heads,)),
     ]
 
 
@@ -422,7 +464,7 @@
     rows = query.shape[0]
     flat = rows * GROUP
     low = jnp.bfloat16
-    vmem, smem = pl.BlockSpec(memory_space=pltpu.VMEM), pl.BlockSpec(memory_space=pltpu.SMEM)
+    vmem, hbm = pl.BlockSpec(memory_space=pltpu.VMEM), pl.BlockSpec(memory_space=pltpu.HBM)
     d_query, d_key, d_value = pl.pallas_call(
         functools.partial(fused_kernel, n, heads),
         out_shape=[
@@ -430,9 +472,9 @@
             jax.ShapeDtypeStruct(key.shape, low),
             jax.ShapeDtypeStruct(value.shape, low),
         ],
-        in_specs=[vmem] * 4 + [smem] * 2,
+        in_specs=[hbm] * 6,
         out_specs=[vmem] * 3,
-        scratch_shapes=fused_scratch(n, heads, rows),
+        scratch_shapes=fused_scratch(n, heads, rows, seg_blocks.shape[0]),
         cost_estimate=pl.CostEstimate(
             flops=10 * n * rows * flat * DH, bytes_accessed=6 * flat * DH, transcendentals=n * rows * flat
         ),

time: 45.7 us -> 41.2 us (0.902)
  local copies, waits for them, and re-layouts: 6 us -> 3.06 us
  Pallas kernels: 38.7 us -> 37.3 us
    unnamed x15 -> x7, local copies, waits for them, and re-layouts: 6 us -> 3.06 us
    pallas_call x1, Pallas kernels: 38.7 us -> 37.3 us  [fused_body(): pl.pallas_call(functools.partial(fused_kernel, n, heads), out_shape=[jax....]
where the time goes in v2:
time: 41.2 us; the launch traced here: 41 us
  Pallas kernels  37.3 us (91%)
  local copies, waits for them, and re-layouts  3.06 us (7%)
  between operations  0.65 us (2%)
    pallas_call x1, Pallas kernels, fused_body(): pl.pallas_call(functools.partial(fused_kernel, n, heads), out_shape=[jax....  37.3 us
    unnamed x7, local copies, waits for them, and re-layouts  3.06 us

profile of v2, /device:TPU:0, one launch (start us, length us, event | category | flops | bytes accessed | tf_op | source)
XLA Modules:
  0.0 41.0 jit_solution(13787424198221252313)
XLA Ops:
  0.6 37.3 %shard_map.85 = (bf16[1024,128]{1,0:T(8,128)(2,1)}, bf16[32,4,128]{2,1,0:T(4,128)(2,1)}, bf16[32,4,128]{2,1,0:T(4,128)(2,1)}) custom-call(bf16[1024,128]{1,0:T(8,128)(2,1)} %bitcast.4, bf16[1024,128]{1,0:T(8,128)(2,1)} %bitcast.5, bf16[32,4,128]{2,1,0:T(4,128)(2,1)} %k_hbm.1, bf16[32,4,128]{2,1,0:T(4,128)(2,1)} %v_hbm.1, s32[4]{0:T(128)} %blocks_hbm.1, ...), custom_call_target="tpu_custom_call" | custom-call | flops 1342177280 | bytes 786432 | tf_op jit(solution)/shard_map/pallas_call | solution.py:468
  37.9 0.0 copy-start.1
  38.0 1.7 %copy.12 = bf16[128,8,128]{2,1,0:T(8,128)(2,1)} copy(bf16[128,8,128]{2,1,0:T(8,128)(2,1)} %bitcast.3) | data formatting | bytes 524288
  39.6 0.0 copy-done.1
  39.6 0.0 copy-start
  39.6 0.6 %copy.13 = bf16[32,4,128]{2,1,0:T(4,128)(2,1)} copy(bf16[32,4,128]{2,1,0:T(4,128)(2,1)S(1)} %copy-done.1) | data formatting | bytes 65536
  40.2 0.2 copy-done
  40.4 0.6 %copy.14 = bf16[32,4,128]{2,1,0:T(4,128)(2,1)} copy(bf16[32,4,128]{2,1,0:T(4,128)(2,1)S(1)} %copy-done) | data formatting | bytes 65536
Async XLA Ops:
  37.9 1.7 %copy-start.1 = (bf16[32,4,128]{2,1,0:T(4,128)(2,1)S(1)}, bf16[32,4,128]{2,1,0:T(4,128)(2,1)}, u32[]{:S(2)}) copy-start(bf16[32,4,128]{2,1,0:T(4,128)(2,1)} %get-tuple-element.13) | copy-start | bytes 98308
  39.6 0.8 %copy-start = (bf16[32,4,128]{2,1,0:T(4,128)(2,1)S(1)}, bf16[32,4,128]{2,1,0:T(4,128)(2,1)}, u32[]{:S(2)}) copy-start(bf16[32,4,128]{2,1,0:T(4,128)(2,1)} %get-tuple-element.14) | copy-start | bytes 98308

commit v3 on v2

--- a/solution.py
+++ b/solution.py
@@ -11,6 +11,7 @@
 MESH = pl.DeviceIdType.MESH
 VMEM_BUDGET = 60 * 2**20
 ROW_CHUNK = 256
+OUTER = 2.0**-4
 
 DH = 128
 GROUP = 8
@@ -207,6 +208,7 @@
     part = rows // heads
     scale = 1.0 / math.sqrt(DH)
     power = scale * math.log2(math.e)
+    inner = scale / OUTER
     chunk = min(ROW_CHUNK, rows_flat)
     chunks = [slice(r, r + chunk) for r in range(0, rows_flat, chunk)]
 
@@ -303,6 +305,8 @@
         chain_arrival(0, dh).wait_recv()
     relay_copy(0).start()
 
+    key_pos = lax.broadcasted_iota(jnp.int32, (rows, 1), 0)
+
     def stats_step(t, carry):
         d = t // 2
         own_column = lax.rem(t, 2) == 0
@@ -319,18 +323,23 @@
             relay_arrival(d).wait_recv()
 
         keys, values = kv[slot, 0], kv[slot, 1]
-        key_pos = slot * rows + lax.broadcasted_iota(jnp.int32, (rows, 1), 0)
+        s_all = jnp.dot(keys, q_turned[...], preferred_element_type=jnp.float32)
+        dp_all = jnp.dot(values, do_turned[...], preferred_element_type=jnp.float32)
+        bound = limit - slot * rows
+        found = []
         for c in chunks:
-            s = jnp.dot(keys, q_turned[:, c], preferred_element_type=jnp.float32)
-            s = jnp.where(key_pos < limit[:, c], s, NEG)
+            s = jnp.where(key_pos < bound[:, c], s_all[:, c], NEG)
             high = jnp.max(s, axis=0, keepdims=True)
             p = jnp.exp2((s - high) * power)
-            dp = jnp.dot(values, do_turned[:, c], preferred_element_type=jnp.float32)
+            total = jnp.sum(p, axis=0, keepdims=True)
+            weighted = jnp.sum(p * dp_all[:, c], axis=0, keepdims=True)
+            found.append((p, high, total, weighted))
+        dp_s[slot] = dp_all
+        for c, (p, high, total, weighted) in zip(chunks, found):
             p_s[slot, :, c] = p
-            dp_s[slot, :, c] = dp
             m_s[slot, :, c] = high
-            l_s[slot, :, c] = jnp.sum(p, axis=0, keepdims=True)
-            w_s[slot, :, c] = jnp.sum(p * dp, axis=0, keepdims=True)
+            l_s[slot, :, c] = total
+            w_s[slot, :, c] = weighted
         return carry
 
     lax.fori_loop(0, n, stats_step, 0)
@@ -368,14 +377,15 @@
         d = lax.rem(t // 2 + 1, chain)
         other_column = lax.rem(t, 2) == 0
         slot = 2 * down(d) + lax.rem(b + t + 1, 2)
-        key_part = jnp.zeros((rows, DH), jnp.float32)
-        value_part = jnp.zeros((rows, DH), jnp.float32)
+        probs_low, ds = [], []
         for c in chunks:
             probs = p_s[slot, :, c] * m_s[slot, :, c]
-            ds = (probs * (dp_s[slot, :, c] - delta[:, c])).astype(jnp.bfloat16)
-            ds_s[slot, :, c] = ds
-            value_part += jnp.dot(probs.astype(jnp.bfloat16), do_ref[c, :], preferred_element_type=jnp.float32)
-            key_part += jnp.dot(ds, q_ref[c, :], preferred_element_type=jnp.float32)
+            probs_low.append(probs.astype(jnp.bfloat16))
+            ds.append((probs * (dp_s[slot, :, c] - delta[:, c])).astype(jnp.bfloat16))
+        probs_low, ds = jnp.concatenate(probs_low, axis=1), jnp.concatenate(ds, axis=1)
+        value_part = jnp.dot(probs_low, do_ref[...], preferred_element_type=jnp.float32)
+        key_part = jnp.dot(ds, q_ref[...], preferred_element_type=jnp.float32)
+        ds_s[slot] = ds
 
         @pl.when(other_column)
         def _():
@@ -403,7 +413,7 @@
 
     def query_rows(c):
         all_ds = ds_s[:, :, c].reshape(n * rows, c.stop - c.start)
-        dq_ref[c, :] = (contract_first(all_keys, all_ds) * scale).T.astype(jnp.bfloat16)
+        dq_ref[c, :] = (contract_first(all_keys, all_ds) * inner).T.astype(jnp.bfloat16)
 
     middle = rows_flat // 2
     query_rows(slice(0, middle))
@@ -419,8 +429,8 @@
         acc = gz_in[i].astype(jnp.float32)
         for source in range(1, chain):
             acc = acc + gz_in[source * heads + i].astype(jnp.float32)
-        dk_ref[:, i, :] = (acc[0] * scale).astype(jnp.bfloat16)
-        dv_ref[:, i, :] = acc[1].astype(jnp.bfloat16)
+        dk_ref[:, i, :] = (acc[0] * inner).astype(jnp.bfloat16)
+        dv_ref[:, i, :] = (acc[1] / OUTER).astype(jnp.bfloat16)
 
     for da, dh in others:
         chain_copy(da, dh).wait_send()
@@ -482,7 +492,8 @@
             collective_id=0, has_side_effects=True, vmem_limit_bytes=VMEM_BUDGET
         ),
     )(query.reshape(flat, DH), d_out.reshape(flat, DH), key, value, seg_blocks, seg_audio)
-    return d_query.reshape(query.shape), d_key, d_value
+    d_query = d_query.reshape(query.shape)
+    return tuple(grad * jnp.asarray(OUTER, low) for grad in (d_query, d_key, d_value))
 
 
 def plan_body(n, heads, query, key, value, d_out, seg_blocks, seg_audio):

time: 41.2 us -> 40.4 us (0.981)
  local copies, waits for them, and re-layouts: 3.06 us -> 0.01 us
  other arithmetic: 0 us -> 2.34 us
    unnamed x7 -> x4, local copies, waits for them, and re-layouts: 3.06 us -> 0.01 us
    mul x0 -> x2, other arithmetic: none -> 2.34 us  [fused_body(): grad * jnp.asarray(OUTER, low)]
where the time goes in v3:
time: 40.4 us; the launch traced here: 40.2 us
  Pallas kernels  37.2 us (92%)
  other arithmetic  2.34 us (6%)
  between operations  0.66 us (2%)
    pallas_call x1, Pallas kernels, fused_body(): pl.pallas_call(functools.partial(fused_kernel, n, heads), out_shape=[jax....  37.2 us
    mul x2, other arithmetic, fused_body(): grad * jnp.asarray(OUTER, low)  2.34 us

profile of v3, /device:TPU:0, one launch (start us, length us, event | category | flops | bytes accessed | tf_op | source)
XLA Modules:
  0.0 40.2 jit_solution(3676796353204115367)
XLA Ops:
  0.6 37.2 %shard_map.85 = (bf16[1024,128]{1,0:T(8,128)(2,1)}, bf16[32,4,128]{2,1,0:T(4,128)(2,1)}, bf16[32,4,128]{2,1,0:T(4,128)(2,1)}) custom-call(bf16[1024,128]{1,0:T(8,128)(2,1)} %bitcast.4, bf16[1024,128]{1,0:T(8,128)(2,1)} %bitcast.5, bf16[32,4,128]{2,1,0:T(4,128)(2,1)} %k_hbm.1, bf16[32,4,128]{2,1,0:T(4,128)(2,1)} %v_hbm.1, s32[4]{0:T(128)} %blocks_hbm.1, ...), custom_call_target="tpu_custom_call" | custom-call | flops 1342177280 | bytes 786432 | tf_op jit(solution)/shard_map/pallas_call | solution.py:478
  37.9 0.0 copy-start
  37.9 0.0 copy-start.1
  37.9 1.7 %multiply_bitcast_fusion = bf16[128,8,128]{2,1,0:T(8,128)(2,1)} fusion(bf16[1024,128]{1,0:T(8,128)(2,1)} %get-tuple-element.6), kind=kLoop, calls=%fused_computation | loop fusion | flops 131072 | bytes 524288 | tf_op jit(solution)/shard_map/mul | solution.py:496
  39.6 0.0 copy-done
  39.6 0.0 copy-done.1
  39.6 0.7 %broadcast_multiply_fusion = (bf16[32,4,128]{2,1,0:T(4,128)(2,1)}, bf16[32,4,128]{2,1,0:T(4,128)(2,1)}) fusion(bf16[32,4,128]{2,1,0:T(4,128)(2,1)S(1)} %copy-done.1, bf16[32,4,128]{2,1,0:T(4,128)(2,1)S(1)} %copy-done), kind=kLoop, calls=%fused_computation.1 | loop fusion | flops 32768 | bytes 131072 | tf_op jit(solution)/shard_map/mul | solution.py:496
Async XLA Ops:
  37.9 1.7 %copy-start = (bf16[32,4,128]{2,1,0:T(4,128)(2,1)S(1)}, bf16[32,4,128]{2,1,0:T(4,128)(2,1)}, u32[]{:S(2)}) copy-start(bf16[32,4,128]{2,1,0:T(4,128)(2,1)} %get-tuple-element.7) | copy-start | bytes 98308
  37.9 1.7 %copy-start.1 = (bf16[32,4,128]{2,1,0:T(4,128)(2,1)S(1)}, bf16[32,4,128]{2,1,0:T(4,128)(2,1)}, u32[]{:S(2)}) copy-start(bf16[32,4,128]{2,1,0:T(4,128)(2,1)} %get-tuple-element.8) | copy-start | bytes 98308

commit v4 on v3

--- a/solution.py
+++ b/solution.py
@@ -308,9 +308,9 @@
     key_pos = lax.broadcasted_iota(jnp.int32, (rows, 1), 0)
 
     def stats_step(t, carry):
-        d = t // 2
-        own_column = lax.rem(t, 2) == 0
-        slot = 2 * down(d) + lax.rem(b + t, 2)
+        d = lax.rem(t, chain)
+        own_column = t < chain
+        slot = 2 * down(d) + lax.rem(b + t // chain, 2)
 
         @pl.when(own_column & (t > 0))
         def _():
@@ -374,9 +374,9 @@
         return own_part[d] + gy_in[down(d)].astype(jnp.float32)
 
     def grad_step(t, carry):
-        d = lax.rem(t // 2 + 1, chain)
-        other_column = lax.rem(t, 2) == 0
-        slot = 2 * down(d) + lax.rem(b + t + 1, 2)
+        d = chain - 1 - lax.rem(t, chain)
+        other_column = t < chain
+        slot = 2 * down(d) + lax.rem(b + t // chain + 1, 2)
         probs_low, ds = [], []
         for c in chunks:
             probs = p_s[slot, :, c] * m_s[slot, :, c]
@@ -398,12 +398,11 @@
             own_part[d, 0] = key_part
             own_part[d, 1] = value_part
 
-        @pl.when(jnp.logical_not(other_column) & (t > 1))
+        @pl.when(jnp.logical_not(other_column) & (d > 0))
         def _():
-            before = t // 2
-            gz_out[before] = combine(before).astype(jnp.bfloat16)
+            gz_out[d] = combine(d).astype(jnp.bfloat16)
             for dh in range(heads):
-                sum_copy(before, dh).start()
+                sum_copy(d, dh).start()
 
         return carry
 

time: 40.4 us -> 33.6 us (0.83)
  Pallas kernels: 37.2 us -> 30.4 us
    pallas_call x1, Pallas kernels: 37.2 us -> 30.4 us  [fused_body(): pl.pallas_call(functools.partial(fused_kernel, n, heads), out_shape=[jax....]
where the time goes in v4:
time: 33.6 us; the launch traced here: 33.4 us
  Pallas kernels  30.4 us (90%)
  other arithmetic  2.34 us (7%)
  between operations  0.66 us (2%)
    pallas_call x1, Pallas kernels, fused_body(): pl.pallas_call(functools.partial(fused_kernel, n, heads), out_shape=[jax....  30.4 us
    mul x2, other arithmetic, fused_body(): grad * jnp.asarray(OUTER, low)  2.34 us

profile of v4, /device:TPU:0, one launch (start us, length us, event | category | flops | bytes accessed | tf_op | source)
XLA Modules:
  0.0 33.4 jit_solution(18356989438001727341)
XLA Ops:
  0.6 30.4 %shard_map.85 = (bf16[1024,128]{1,0:T(8,128)(2,1)}, bf16[32,4,128]{2,1,0:T(4,128)(2,1)}, bf16[32,4,128]{2,1,0:T(4,128)(2,1)}) custom-call(bf16[1024,128]{1,0:T(8,128)(2,1)} %bitcast.4, bf16[1024,128]{1,0:T(8,128)(2,1)} %bitcast.5, bf16[32,4,128]{2,1,0:T(4,128)(2,1)} %k_hbm.1, bf16[32,4,128]{2,1,0:T(4,128)(2,1)} %v_hbm.1, s32[4]{0:T(128)} %blocks_hbm.1, ...), custom_call_target="tpu_custom_call" | custom-call | flops 1342177280 | bytes 786432 | tf_op jit(solution)/shard_map/pallas_call | solution.py:477
  31.1 0.0 copy-start
  31.1 0.0 copy-start.1
  31.1 1.7 %multiply_bitcast_fusion = bf16[128,8,128]{2,1,0:T(8,128)(2,1)} fusion(bf16[1024,128]{1,0:T(8,128)(2,1)} %get-tuple-element.6), kind=kLoop, calls=%fused_computation | loop fusion | flops 131072 | bytes 524288 | tf_op jit(solution)/shard_map/mul | solution.py:495
  32.8 0.0 copy-done
  32.8 0.0 copy-done.1
  32.8 0.7 %broadcast_multiply_fusion = (bf16[32,4,128]{2,1,0:T(4,128)(2,1)}, bf16[32,4,128]{2,1,0:T(4,128)(2,1)}) fusion(bf16[32,4,128]{2,1,0:T(4,128)(2,1)S(1)} %copy-done.1, bf16[32,4,128]{2,1,0:T(4,128)(2,1)S(1)} %copy-done), kind=kLoop, calls=%fused_computation.1 | loop fusion | flops 32768 | bytes 131072 | tf_op jit(solution)/shard_map/mul | solution.py:495
Async XLA Ops:
  31.1 1.7 %copy-start = (bf16[32,4,128]{2,1,0:T(4,128)(2,1)S(1)}, bf16[32,4,128]{2,1,0:T(4,128)(2,1)}, u32[]{:S(2)}) copy-start(bf16[32,4,128]{2,1,0:T(4,128)(2,1)} %get-tuple-element.7) | copy-start | bytes 98308
  31.1 1.7 %copy-start.1 = (bf16[32,4,128]{2,1,0:T(4,128)(2,1)S(1)}, bf16[32,4,128]{2,1,0:T(4,128)(2,1)}, u32[]{:S(2)}) copy-start(bf16[32,4,128]{2,1,0:T(4,128)(2,1)} %get-tuple-element.8) | copy-start | bytes 98308
